TPU v7x, 128 devices: a whole 4x4x4 slice. The times are simulated.
128 devices in a mesh: row: 8 (over y, core), col: 16 (over x, z).
Axes of the slice: x: 4, y: 4, z: 4, core: 2. Of those that a mesh axis runs over, the one named last changes fastest.
Arguments:
- covariance: float32 [4, 4096, 2, 8192], P(None, 'row', None, 'col'), may hold values from 0 to 2, as said below
- band_mask: int32 [32, 32], replicated, may hold values from 0 to 1, as said below
Outputs:
- schur: float32 [4, 4096, 2, 8192], P(None, 'row', None, 'col')
- panels: float32 [4, 4096, 1024], P(None, 'row')
Inputs may be any that keep to these rules, and one draw needn't show every extreme that they name: band_mask is symmetric, holds 0 or 1, and is 1 wherever the two tile indices differ by at most 1 and wherever either tile index is below 2. covariance is symmetric, with 1 added on its diagonal; A is positive definite.
All inputs are finite; a program needn't handle non-finite values.
Results may differ from a plain program's by a relative error of at most 0.0003.
Values sent between devices are 32-bit elements; how exact they have to be, the bound alone decides.
A program may use at most 128 MiB of HBM per device.

v0:
```python
import jax
import jax.numpy as jnp
from jax import lax
from jax.sharding import PartitionSpec as P

TILE = 512


def from_root(value, axis, root):
    mine = lax.axis_index(axis) == root
    return lax.psum(jnp.where(mine, value, jnp.zeros_like(value)), axis)


def solve_below(factor, column, tile_ids, index):
    count = column.shape[0]
    rhs_block = jnp.transpose(column, (2, 0, 1)).reshape(TILE, count * TILE)
    solved = lax.linalg.triangular_solve(factor, rhs_block, left_side=True, lower=True)
    solved = jnp.transpose(solved.reshape(TILE, count, TILE), (1, 2, 0))
    chosen = tile_ids[:, None, None]
    return jnp.where(
        chosen > index, solved, jnp.where(chosen == index, factor[None], jnp.zeros_like(solved))
    )


def outer_update(target, row_part, col_part):
    return target - jnp.einsum("mab,ncb->manc", row_part, col_part, precision=lax.Precision.HIGHEST)


def body(covariance, band_mask):
    row_count = lax.axis_size("row")
    col_count = lax.axis_size("col")
    row_index = lax.axis_index("row")
    col_index = lax.axis_index("col")
    tile_total = band_mask.shape[0]
    row_tiles = tile_total // row_count
    col_tiles = tile_total // col_count
    row_ids = jnp.arange(row_tiles, dtype=jnp.int32) * row_count + row_index
    col_ids = jnp.arange(col_tiles, dtype=jnp.int32) * col_count + col_index
    keep_all = band_mask.astype(jnp.float32)
    keep_rows = lax.dynamic_index_in_dim(
        keep_all.reshape(row_tiles, row_count, tile_total), row_index, 1, keepdims=False
    )
    keep_local = lax.dynamic_index_in_dim(
        keep_rows.reshape(row_tiles, col_tiles, col_count), col_index, 2, keepdims=False
    )
    schur = covariance * keep_local[:, None, :, None]

    def to_columns(row_part):
        grouped = row_part.reshape(col_tiles, col_count // row_count, TILE, TILE)
        picked = lax.dynamic_index_in_dim(grouped, col_index // row_count, 1, keepdims=False)
        return from_root(picked, "row", col_index % row_count)

    def make_panel(column, column_step):
        diag_local = column[column_step // row_count]
        received = from_root(diag_local, "row", column_step % row_count)
        identity = jnp.eye(TILE, dtype=jnp.float32)
        diagonal = jnp.where(col_index == column_step % col_count, received, identity)
        factor = jnp.linalg.cholesky(diagonal)
        panel = solve_below(factor, column, row_ids, column_step)
        row_part = from_root(panel, "col", column_step % col_count)
        return (row_part, to_columns(row_part))

    rows_zero, cols_zero = make_panel(schur[:, :, 0, :], 0)
    schur = outer_update(schur, rows_zero, cols_zero)
    rows_one, cols_one = make_panel(schur[:, :, 0, :], 1)
    schur = outer_update(schur, rows_one, cols_one)
    row_keep = (row_ids >= 2).astype(jnp.float32)
    col_keep = (col_ids >= 2).astype(jnp.float32)
    schur = schur * row_keep[:, None, None, None] * col_keep[None, None, :, None]
    panels = jnp.concatenate([rows_zero, rows_one], axis=2)
    return (schur, panels)


def solution(mesh):
    return jax.shard_map(
        body,
        mesh=mesh,
        in_specs=(P(None, "row", None, "col"), P()),
        out_specs=(P(None, "row", None, "col"), P(None, "row", None)),
        check_vma=False,
    )
```

profile of v0, /device:TPU:0, one launch (start us, length us, event | category | flops | bytes accessed | tf_op | source)
XLA Modules:
  0.0 887.7 jit_solution(13052598460974647819)
XLA Ops:
  8.3 13.1 %copy.18 = f32[4,512,2,512]{1,3,2,0:T(8,128)} copy(f32[4,512,2,512]{3,2,1,0:T(2,128)} %param.5) | data formatting | bytes 16777216 | tf_op args[0]
  21.4 4.5 broadcast_multiply_fusion
  25.9 3.4 copy-done.1
  29.3 1.1 fusion.42
  30.5 4.6 slice_bitcast_fusion.1
  35.1 5.4 copy.20
  40.6 54.9 %all-reduce.8.cloned.1.call-done = f32[512,512]{0,1:T(8,128)} async-done(((f32[512,512]{0,1:T(8,128)}), f32[512,512]{0,1:T(8,128)}) %all-reduce.8.cloned.1.call-update) | async-done | bytes 1048592 | tf_op jit(solution)/shard_map/psum | solution.py:11
  95.5 1.4 convert_select_fusion.1
  97.6 11.7 %cholesky.286 = f32[128,128]{1,0:T(8,128)S(1)} custom-call(f32[128,128]{1,0:T(8,128)S(1)} %cholesky.426), custom_call_target="Cholesky" | custom-call | tf_op jit(solution)/shard_map/jit(cholesky)/cholesky | solution.py:58
  109.3 9.8 %custom-call.27 = f32[1,128,128]{1,2,0:T(8,128)S(1)} custom-call(f32[1,128,128]{2,1,0:T(8,128)S(1)} %get-tuple-element.67), custom_call_target="InvertDiagBlocksLowerTriangular" | custom-call | tf_op jit(solution)/shard_map/jit(cholesky)/cholesky | solution.py:58
  119.9 11.7 %cholesky.305 = f32[128,128]{1,0:T(8,128)S(1)} custom-call(f32[128,128]{1,0:T(8,128)S(1)} %cholesky.430), custom_call_target="Cholesky" | custom-call | tf_op jit(solution)/shard_map/jit(cholesky)/cholesky | solution.py:58
  131.7 10.2 %custom-call.28 = f32[1,128,128]{1,2,0:T(8,128)S(1)} custom-call(f32[1,128,128]{2,1,0:T(8,128)S(1)} %get-tuple-element.64), custom_call_target="InvertDiagBlocksLowerTriangular" | custom-call | tf_op jit(solution)/shard_map/jit(cholesky)/cholesky | solution.py:58
  142.6 11.7 %cholesky.326 = f32[128,128]{1,0:T(8,128)S(1)} custom-call(f32[128,128]{1,0:T(8,128)S(1)} %cholesky.435), custom_call_target="Cholesky" | custom-call | tf_op jit(solution)/shard_map/jit(cholesky)/cholesky | solution.py:58
  155.0 9.8 %custom-call.29 = f32[1,128,128]{1,2,0:T(8,128)S(1)} custom-call(f32[1,128,128]{2,1,0:T(8,128)S(1)} %get-tuple-element.61), custom_call_target="InvertDiagBlocksLowerTriangular" | custom-call | tf_op jit(solution)/shard_map/jit(cholesky)/cholesky | solution.py:58
  165.4 11.7 %cholesky.343 = f32[128,128]{1,0:T(8,128)S(1)} custom-call(f32[128,128]{1,0:T(8,128)S(1)} %convolution_subtract_fusion.9), custom_call_target="Cholesky" | custom-call | tf_op jit(solution)/shard_map/jit(cholesky)/cholesky | solution.py:58
  181.6 7.9 while.4
  182.2 1.4 bitcast_dynamic-update-slice_fusion.4
  184.2 1.4 bitcast_dynamic-update-slice_fusion.4
  186.1 1.4 bitcast_dynamic-update-slice_fusion.4
  188.1 1.4 bitcast_dynamic-update-slice_fusion.4
  189.5 39.3 %custom-call.30 = f32[4,128,128]{1,2,0:T(8,128)S(1)} custom-call(f32[4,128,128]{2,1,0:T(8,128)S(1)} %get-tuple-element.18), custom_call_target="InvertDiagBlocksLowerTriangular" | custom-call | tf_op jit(solution)/shard_map/triangular_solve/custom-call.3 | solution.py:17
  228.8 2.4 fusion.40
  231.2 3.0 convolution_subtract_fusion.3
  235.4 3.5 convolution_subtract_fusion.1
  238.9 1.1 fusion.71
  240.0 5.6 fusion.24
  246.6 2.5 pad_maximum_fusion.1
  249.2 5.3 copy.34
  254.5 4.9 select_select_fusion.1
  259.5 102.4 %all-reduce.10.cloned.1.call-done = f32[4,512,512]{2,1,0:T(8,128)} async-done(((f32[4,512,512]{2,1,0:T(8,128)}), f32[4,512,512]{2,1,0:T(8,128)}) %all-reduce.10.cloned.1.call-update) | async-done | bytes 4194320 | tf_op jit(solution)/shard_map/psum | solution.py:11
  362.0 3.1 fusion.34
  365.2 65.4 %all-reduce.12.cloned.1.call-done = f32[2,512,512]{2,1,0:T(8,128)} async-done(((f32[2,512,512]{2,1,0:T(8,128)}), f32[2,512,512]{2,1,0:T(8,128)}) %all-reduce.12.cloned.1.call-update) | async-done | bytes 2097168 | tf_op jit(solution)/shard_map/psum | solution.py:11
  430.6 16.9 %fusion.18 = f32[4,512,2,512]{1,3,2,0:T(8,128)S(1)} fusion(f32[4,512,2,512]{1,3,2,0:T(8,128)} %copy-done.1, f32[4,512,512]{2,1,0:T(8,128)} %all-reduce.10.cloned.1.call-done, f32[2,512,512]{2,1,0:T(8,128)} %all-reduce.12.cloned.1.call-done), kind=kOutput, calls=%fused_computation.29 | convolution fusion | flops 12886999040 | bytes 23068672 | tf_op jit(solution)/shard_map/mab,ncb->manc/dot_general | solution.py:26
  447.5 3.4 copy-done
  452.1 4.6 slice_bitcast_fusion
  456.7 5.6 copy.25
  462.4 51.8 %all-reduce.14.cloned.1.call-done = f32[512,512]{0,1:T(8,128)} async-done(((f32[512,512]{0,1:T(8,128)}), f32[512,512]{0,1:T(8,128)}) %all-reduce.14.cloned.1.call-update) | async-done | bytes 1048592 | tf_op jit(solution)/shard_map/psum | solution.py:11
  515.6 11.7 %cholesky.358 = f32[128,128]{1,0:T(8,128)S(1)} custom-call(f32[128,128]{1,0:T(8,128)S(1)} %cholesky.439), custom_call_target="Cholesky" | custom-call | tf_op jit(solution)/shard_map/jit(cholesky)/cholesky | solution.py:58
  528.0 9.8 %custom-call.31 = f32[1,128,128]{1,2,0:T(8,128)S(1)} custom-call(f32[1,128,128]{2,1,0:T(8,128)S(1)} %get-tuple-element.57), custom_call_target="InvertDiagBlocksLowerTriangular" | custom-call | tf_op jit(solution)/shard_map/jit(cholesky)/cholesky | solution.py:58
  538.6 11.7 %cholesky.377 = f32[128,128]{1,0:T(8,128)S(1)} custom-call(f32[128,128]{1,0:T(8,128)S(1)} %cholesky.443), custom_call_target="Cholesky" | custom-call | tf_op jit(solution)/shard_map/jit(cholesky)/cholesky | solution.py:58
  551.0 10.0 %custom-call.32 = f32[1,128,128]{1,2,0:T(8,128)S(1)} custom-call(f32[1,128,128]{2,1,0:T(8,128)S(1)} %get-tuple-element.54), custom_call_target="InvertDiagBlocksLowerTriangular" | custom-call | tf_op jit(solution)/shard_map/jit(cholesky)/cholesky | solution.py:58
  561.6 11.7 %cholesky.398 = f32[128,128]{1,0:T(8,128)S(1)} custom-call(f32[128,128]{1,0:T(8,128)S(1)} %cholesky.448), custom_call_target="Cholesky" | custom-call | tf_op jit(solution)/shard_map/jit(cholesky)/cholesky | solution.py:58
  574.0 9.8 %custom-call.33 = f32[1,128,128]{1,2,0:T(8,128)S(1)} custom-call(f32[1,128,128]{2,1,0:T(8,128)S(1)} %get-tuple-element.51), custom_call_target="InvertDiagBlocksLowerTriangular" | custom-call | tf_op jit(solution)/shard_map/jit(cholesky)/cholesky | solution.py:58
  584.4 11.7 %cholesky.415 = f32[128,128]{1,0:T(8,128)S(1)} custom-call(f32[128,128]{1,0:T(8,128)S(1)} %convolution_subtract_fusion.8), custom_call_target="Cholesky" | custom-call | tf_op jit(solution)/shard_map/jit(cholesky)/cholesky | solution.py:58
  599.7 7.7 while.5
  600.3 1.3 bitcast_dynamic-update-slice_fusion.5
  602.3 1.3 bitcast_dynamic-update-slice_fusion.5
  604.2 1.3 bitcast_dynamic-update-slice_fusion.5
  606.1 1.3 bitcast_dynamic-update-slice_fusion.5
  607.4 39.3 %custom-call.34 = f32[4,128,128]{1,2,0:T(8,128)S(1)} custom-call(f32[4,128,128]{2,1,0:T(8,128)S(1)} %get-tuple-element.19), custom_call_target="InvertDiagBlocksLowerTriangular" | custom-call | tf_op jit(solution)/shard_map/triangular_solve/custom-call.3 | solution.py:17
  646.8 2.4 fusion.37
  649.2 3.0 convolution_subtract_fusion.2
  653.3 3.5 convolution_subtract_fusion
  656.9 1.1 fusion.65
  658.0 5.6 fusion.21
  664.7 2.5 pad_maximum_fusion.2
  667.2 5.3 copy.26
  672.5 4.9 select_select_fusion
  677.5 103.0 %all-reduce.16.cloned.1.call-done = f32[4,512,512]{2,1,0:T(8,128)} async-done(((f32[4,512,512]{2,1,0:T(8,128)}), f32[4,512,512]{2,1,0:T(8,128)}) %all-reduce.16.cloned.1.call-update) | async-done | bytes 4194320 | tf_op jit(solution)/shard_map/psum | solution.py:11
  780.5 3.1 fusion.33
  783.7 8.3 pad_maximum_fusion
  792.1 57.1 %all-reduce.18.cloned.1.call-done = f32[2,512,512]{2,1,0:T(8,128)} async-done(((f32[2,512,512]{2,1,0:T(8,128)}), f32[2,512,512]{2,1,0:T(8,128)}) %all-reduce.18.cloned.1.call-update) | async-done | bytes 2097168 | tf_op jit(solution)/shard_map/psum | solution.py:11
  849.2 18.1 %multiply_multiply_fusion = f32[4,512,2,512]{1,3,2,0:T(8,128)} fusion(f32[4,512,2,512]{1,3,2,0:T(8,128)} %copy-done, f32[2]{0:T(128)S(1)} %compare_convert_fusion, f32[4]{0:T(128)S(1)} %compare_convert_fusion.1, f32[4,512,512]{2,1,0:T(8,128)} %all-reduce.16.cloned.1.call-done, f32[2,512,512]{2,1,0:T(8,128)} %all-reduce.18.cloned.1.call-done), kind=kOutput, calls=%fused_computation.5 | convolution fusion | flops 12891193344 | bytes 23068696 | tf_op jit(solution)/shard_map/mab,ncb->manc/dot_general | solution.py:26
  867.3 13.1 %copy.29 = f32[4,512,2,512]{3,2,1,0:T(2,128)} copy(f32[4,512,2,512]{1,3,2,0:T(8,128)} %multiply_multiply_fusion) | data formatting | bytes 16777216
  (99 shorter events, 23.5 us)
Async XLA Ops:
  7.2 88.3 %all-reduce.8.cloned.1.call-start = ((), (), s32[]{:S(2)}) async-start(), calls=%async_computation | async-start | bytes 2097152 | tf_op jit(solution)/shard_map/psum | solution.py:11
  25.9 3.4 copy-start.1
  30.4 331.5 %all-reduce.10.cloned.1.call-start = ((), (), s32[]{:S(2)}) async-start(), calls=%async_computation.1 | async-start | bytes 8388608 | tf_op jit(solution)/shard_map/psum | solution.py:11
  95.5 1.8 copy-start.4
  228.8 6.6 copy-start.2
  259.5 171.1 %all-reduce.12.cloned.1.call-start = ((), (), s32[]{:S(2)}) async-start(), calls=%async_computation.2 | async-start | bytes 4194304 | tf_op jit(solution)/shard_map/psum | solution.py:11
  365.1 149.0 %all-reduce.14.cloned.1.call-start = ((), (), s32[]{:S(2)}) async-start(), calls=%async_computation.3 | async-start | bytes 2097152 | tf_op jit(solution)/shard_map/psum | solution.py:11
  447.5 3.4 copy-start
  452.0 328.5 %all-reduce.16.cloned.1.call-start = ((), (), s32[]{:S(2)}) async-start(), calls=%async_computation.4 | async-start | bytes 8388608 | tf_op jit(solution)/shard_map/psum | solution.py:11
  514.1 1.2 copy-start.5
  646.8 6.6 copy-start.3
  677.5 171.7 %all-reduce.18.cloned.1.call-start = ((), (), s32[]{:S(2)}) async-start(), calls=%async_computation.5 | async-start | bytes 4194304 | tf_op jit(solution)/shard_map/psum | solution.py:11
Sparse Core Ops, SparseCore 0:
  30.5 64.9 all-reduce.7
  259.6 102.3 all-reduce.9
  365.2 65.3 all-reduce.11
  452.1 61.9 all-reduce.13
  677.6 102.8 all-reduce.15
  783.8 65.3 all-reduce.17
where the time goes:
time: 892 us; the launch traced here: 888 us
  waiting for transfers between devices  435 us (49%)
  other arithmetic  276 us (31%)
  local copies, waits for them, and re-layouts  81.6 us (9%)
  matrix products  74.4 us (8%)
  between operations  20.1 us (2%)
    psum x6, waiting for transfers between devices, from_root(): return lax.psum(jnp.where(mine, value, jnp.zeros_like(value)), axis)  435 us
    another operation x29, other arithmetic, make_panel(): factor = jnp.linalg.cholesky(diagonal)  158 us
    another operation x7, other arithmetic, solve_below(): lax.linalg.triangular_solve(factor, rhs_block, left_side=True, lower=True)  84.2 us
    another operation x14, matrix products, solve_below(): lax.linalg.triangular_solve(factor, rhs_block, left_side=True, lower=True)  35.6 us
    dot_general x2, matrix products, outer_update(): jnp.einsum('mab,ncb->manc', row_part, col_part, precision=lax.Precision.H...  35 us
    unnamed x14, local copies, waits for them, and re-layouts  33.8 us
    another operation x28, local copies, waits for them, and re-layouts, solve_below(): lax.linalg.triangular_solve(factor, rhs_block, left_side=True, lower=True)  20.8 us
    transpose x4, local copies, waits for them, and re-layouts, solve_below(): rhs_block = jnp.transpose(column, (2, 0, 1)).reshape(TILE, count * TILE)  20.4 us
  transfers between devices with their start and end apart: 6, of which 6 were waited for; matrix products, arithmetic and copies ran while one was open for 3% of the time, Pallas kernels for 0%

commit v1 on v0

--- a/solution.py
+++ b/solution.py
@@ -8,7 +8,7 @@
 
 def from_root(value, axis, root):
     mine = lax.axis_index(axis) == root
-    return lax.psum(jnp.where(mine, value, jnp.zeros_like(value)), axis)
+    return jnp.sum(lax.all_gather(jnp.where(mine, value, jnp.zeros_like(value)), axis), axis=0)
 
 
 def solve_below(factor, column, tile_ids, index):

time: 892 us -> 1550 us (1.74)
  waiting for transfers between devices: 435 us -> 970 us
  other arithmetic: 276 us -> 360 us
  matrix products: 74.4 us -> 99.2 us
    all_gather x0 -> x6, waiting for transfers between devices: none -> 970 us  [from_root(): lax.all_gather(jnp.where(mine, value, jnp.zeros_like(value)), axis)]
    psum x6 -> x0, waiting for transfers between devices: 435 us -> none  [from_root(): return lax.psum(jnp.where(mine, value, jnp.zeros_like(value)), axis)]
    reduce_sum x0 -> x6, other arithmetic: none -> 71.4 us  [from_root(): jnp.sum(lax.all_gather(jnp.where(mine, value, jnp.zeros_like(value)), axi...]
    dot_general x2, matrix products: 35 us -> 59.7 us  [outer_update(): jnp.einsum('mab,ncb->manc', row_part, col_part, precision=lax.Precision.H...]
    transpose x4 -> x0, local copies, waits for them, and re-layouts: 20.4 us -> none  [solve_below(): rhs_block = jnp.transpose(column, (2, 0, 1)).reshape(TILE, count * TILE)]
    unnamed x14 -> x12, local copies, waits for them, and re-layouts: 33.8 us -> 44.6 us
where the time goes in v1:
time: 1550 us; the launch traced here: 1530 us
  waiting for transfers between devices  970 us (63%)
  other arithmetic  360 us (23%)
  matrix products  99.2 us (6%)
  local copies, waits for them, and re-layouts  82.7 us (5%)
  between operations  20.2 us (1%)
    all_gather x6, waiting for transfers between devices, from_root(): lax.all_gather(jnp.where(mine, value, jnp.zeros_like(value)), axis)  970 us
    another operation x29, other arithmetic, make_panel(): factor = jnp.linalg.cholesky(diagonal)  170 us
    another operation x7, other arithmetic, solve_below(): lax.linalg.triangular_solve(factor, rhs_block, left_side=True, lower=True)  84.2 us
    reduce_sum x6, other arithmetic, from_root(): jnp.sum(lax.all_gather(jnp.where(mine, value, jnp.zeros_like(value)), axi...  71.4 us
    dot_general x2, matrix products, outer_update(): jnp.einsum('mab,ncb->manc', row_part, col_part, precision=lax.Precision.H...  59.7 us
    unnamed x12, local copies, waits for them, and re-layouts  44.6 us
    another operation x14, matrix products, solve_below(): lax.linalg.triangular_solve(factor, rhs_block, left_side=True, lower=True)  35.8 us
  transfers between devices with their start and end apart: 6, of which 6 were waited for; matrix products, arithmetic and copies ran while one was open for 3% of the time, Pallas kernels for 0%

profile of v1, /device:TPU:0, one launch (start us, length us, event | category | flops | bytes accessed | tf_op | source)
XLA Modules:
  0.0 1533.1 jit_solution(17597565671001925369)
XLA Ops:
  8.3 5.0 copy_multiply_fusion
  13.3 3.4 copy-done
  17.9 4.6 slice.159
  22.6 47.6 %all-gather.13.cloned.1.call-done = f32[8,512,1,512]{3,1,2,0:T(8,128)} async-done(((f32[1,512,1,512]{3,1,2,0:T(8,128)}), f32[8,512,1,512]{3,1,2,0:T(8,128)}) %all-gather.13.cloned.1.call-update) | async-done | bytes 8388624 | tf_op jit(solution)/shard_map/all_gather | solution.py:11
  70.2 4.5 reduce_sum.54
  75.8 11.7 cholesky.286
  87.5 9.8 custom-call.27
  98.2 11.9 cholesky.305
  110.1 9.8 custom-call.28
  120.6 11.7 cholesky.326
  133.1 9.8 custom-call.29
  143.5 23.2 %cholesky.343 = f32[128,128]{1,0:T(8,128)S(1)} custom-call(f32[128,128]{1,0:T(8,128)S(1)} %convolution_subtract_fusion.9), custom_call_target="Cholesky" | custom-call | tf_op jit(solution)/shard_map/jit(cholesky)/cholesky | solution.py:58
  170.9 8.1 while.4
  171.6 1.3 bitcast_dynamic-update-slice_fusion.4
  173.7 1.3 bitcast_dynamic-update-slice_fusion.4
  175.7 1.3 bitcast_dynamic-update-slice_fusion.4
  177.7 1.3 bitcast_dynamic-update-slice_fusion.4
  179.1 39.3 %custom-call.30 = f32[4,128,128]{1,2,0:T(8,128)S(1)} custom-call(f32[4,128,128]{2,1,0:T(8,128)S(1)} %get-tuple-element.18), custom_call_target="InvertDiagBlocksLowerTriangular" | custom-call | tf_op jit(solution)/shard_map/triangular_solve/custom-call.3 | solution.py:17
  218.4 2.4 fusion.37
  220.9 3.0 convolution_subtract_fusion.3
  225.0 3.5 convolution_subtract_fusion.1
  229.6 5.7 fusion.24
  236.5 2.5 pad_maximum_fusion.1
  239.0 5.3 copy.33
  244.3 4.9 select_select_fusion.1
  249.4 369.0 %all-gather.15.cloned.1.call-done = f32[64,512,512]{2,1,0:T(8,128)} async-done(((f32[4,512,512]{2,1,0:T(8,128)}), f32[64,512,512]{2,1,0:T(8,128)}) %all-gather.15.cloned.1.call-update) | async-done | bytes 67108880 | tf_op jit(solution)/shard_map/all_gather | solution.py:11
  618.4 23.1 %reduce_sum.55 = f32[4,512,512]{2,1,0:T(8,128)} reduce(f32[16,4,512,512]{3,2,1,0:T(8,128)} %bitcast.20, f32[]{:T(128)} %constant.163.clone.1), dimensions={0}, to_apply=%region_9.12 | reduce | flops 15728640 | bytes 71303168 | tf_op jit(solution)/shard_map/reduce_sum | solution.py:11
  641.5 3.2 dynamic-slice_select_fusion.1
  644.7 5.4 copy.41
  650.2 79.2 %all-gather.17.cloned.1.call-done = f32[16,1,512,512]{3,2,1,0:T(8,128)} async-done(((f32[2,1,512,512]{3,2,1,0:T(8,128)}), f32[16,1,512,512]{3,2,1,0:T(8,128)}) %all-gather.17.cloned.1.call-update) | async-done | bytes 16777232 | tf_op jit(solution)/shard_map/all_gather | solution.py:11
  729.4 8.1 bitcast_reduce_fusion.1
  737.5 29.5 %fusion.18 = f32[4,512,2,512]{3,1,2,0:T(8,128)S(1)} fusion(f32[4,512,2,512]{3,1,2,0:T(8,128)} %copy-done, f32[4,512,512,1]{1,0,2,3:T(4,128)} %bitcast.136, f32[2,512,512]{2,1,0:T(8,128)S(1)} %bitcast_reduce_fusion.1), kind=kOutput, calls=%fused_computation.29 | convolution fusion | flops 12886999040 | bytes 23068672 | tf_op jit(solution)/shard_map/mab,ncb->manc/dot_general | solution.py:26
  767.0 3.4 copy-done.1
  771.8 4.6 slice.172
  776.5 45.6 %all-gather.19.cloned.1.call-done = f32[8,512,1,512]{3,1,2,0:T(8,128)} async-done(((f32[1,512,1,512]{3,1,2,0:T(8,128)}), f32[8,512,1,512]{3,1,2,0:T(8,128)}) %all-gather.19.cloned.1.call-update) | async-done | bytes 8388624 | tf_op jit(solution)/shard_map/all_gather | solution.py:11
  822.1 4.5 reduce_sum.57
  827.6 11.7 cholesky.358
  839.5 9.8 custom-call.31
  850.0 12.1 cholesky.377
  863.5 9.8 custom-call.32
  873.9 11.7 cholesky.398
  886.3 9.8 custom-call.33
  896.8 11.9 cholesky.415
  912.2 8.1 while.5
  912.9 1.3 bitcast_dynamic-update-slice_fusion.5
  914.9 1.3 bitcast_dynamic-update-slice_fusion.5
  920.3 39.3 %custom-call.34 = f32[4,128,128]{1,2,0:T(8,128)S(1)} custom-call(f32[4,128,128]{2,1,0:T(8,128)S(1)} %get-tuple-element.19), custom_call_target="InvertDiagBlocksLowerTriangular" | custom-call | tf_op jit(solution)/shard_map/triangular_solve/custom-call.3 | solution.py:17
  959.7 2.4 fusion.35
  962.1 3.0 convolution_subtract_fusion.2
  966.2 3.5 convolution_subtract_fusion
  970.9 5.6 fusion.21
  977.5 2.5 pad_maximum_fusion.2
  980.0 5.3 copy.37
  985.4 4.9 select_select_fusion
  990.4 369.0 %all-gather.21.cloned.1.call-done = f32[64,512,512]{2,1,0:T(8,128)} async-done(((f32[4,512,512]{2,1,0:T(8,128)}), f32[64,512,512]{2,1,0:T(8,128)}) %all-gather.21.cloned.1.call-update) | async-done | bytes 67108880 | tf_op jit(solution)/shard_map/all_gather | solution.py:11
  1359.4 23.1 %reduce_sum.58 = f32[4,512,512]{2,1,0:T(8,128)} reduce(f32[16,4,512,512]{3,2,1,0:T(8,128)} %bitcast.43, f32[]{:T(128)} %constant.163.clone.1), dimensions={0}, to_apply=%region_12.15 | reduce | flops 15728640 | bytes 71303168 | tf_op jit(solution)/shard_map/reduce_sum | solution.py:11
  1382.5 3.2 dynamic-slice_select_fusion
  1385.8 5.4 copy.42
  1391.2 9.9 pad_maximum_fusion
  1401.1 9.9 copy.30
  1411.0 59.4 %all-gather.23.cloned.1.call-done = f32[16,1,512,512]{3,2,1,0:T(8,128)} async-done(((f32[2,1,512,512]{3,2,1,0:T(8,128)}), f32[16,1,512,512]{3,2,1,0:T(8,128)}) %all-gather.23.cloned.1.call-update) | async-done | bytes 16777232 | tf_op jit(solution)/shard_map/all_gather | solution.py:11
  1470.5 8.1 bitcast_reduce_fusion
  1478.6 30.3 %multiply_multiply_fusion = f32[4,512,2,512]{3,1,2,0:T(8,128)S(1)} fusion(f32[4,512,2,512]{3,1,2,0:T(8,128)} %copy-done.1, f32[2]{0:T(128)S(1)} %compare_convert_fusion, f32[4]{0:T(128)S(1)} %compare_convert_fusion.1, f32[4,512,512,1]{1,0,2,3:T(4,128)} %bitcast.137, f32[2,512,512]{2,1,0:T(8,128)S(1)} %bitcast_reduce_fusion), kind=kOutput, calls=%fused_computation.8 | convolution fusion | flops 12891193344 | bytes 23068696 | tf_op jit(solution)/shard_map/mab,ncb->manc/dot_general | solution.py:26
  1508.8 17.0 %copy.29 = f32[4,512,2,512]{3,2,1,0:T(2,128)} copy(f32[4,512,2,512]{3,1,2,0:T(8,128)S(1)} %multiply_multiply_fusion) | data formatting | bytes 16777216
  (103 shorter events, 30.2 us)
Async XLA Ops:
  7.2 63.1 %all-gather.13.cloned.1.call-start = ((), (), s32[]{:S(2)}) async-start(), calls=%async_computation | async-start | bytes 9437184 | tf_op jit(solution)/shard_map/all_gather | solution.py:11
  13.3 3.4 copy-start
  17.9 600.5 %all-gather.15.cloned.1.call-start = ((), (), s32[]{:S(2)}) async-start(), calls=%async_computation.1 | async-start | bytes 71303168 | tf_op jit(solution)/shard_map/all_gather | solution.py:11
  218.4 6.6 copy-start.2
  249.3 480.1 %all-gather.17.cloned.1.call-start = ((), (), s32[]{:S(2)}) async-start(), calls=%async_computation.2 | async-start | bytes 18874368 | tf_op jit(solution)/shard_map/all_gather | solution.py:11
  644.7 177.4 %all-gather.19.cloned.1.call-start = ((), (), s32[]{:S(2)}) async-start(), calls=%async_computation.3 | async-start | bytes 9437184 | tf_op jit(solution)/shard_map/all_gather | solution.py:11
  767.0 3.4 copy-start.1
  771.6 587.8 %all-gather.21.cloned.1.call-start = ((), (), s32[]{:S(2)}) async-start(), calls=%async_computation.4 | async-start | bytes 71303168 | tf_op jit(solution)/shard_map/all_gather | solution.py:11
  959.7 6.6 copy-start.3
  990.3 480.1 %all-gather.23.cloned.1.call-start = ((), (), s32[]{:S(2)}) async-start(), calls=%async_computation.5 | async-start | bytes 18874368 | tf_op jit(solution)/shard_map/all_gather | solution.py:11
Sparse Core Ops, SparseCore 0:
  18.0 52.1 all-gather.12
  249.4 368.9 all-gather.14
  644.8 84.5 all-gather.16
  771.7 50.2 all-gather.18
  990.4 368.9 all-gather.20
  1385.9 84.5 all-gather.22
